TPU v7x, 512 devices: a whole 4x8x8 slice. The times are simulated.
512 devices in a mesh: dp: 64 (over y, z), head: 8 (over x, core).
Axes of the slice: x: 4, y: 8, z: 8, core: 2. Of those that a mesh axis runs over, the one named last changes fastest.
Arguments:
- queries: bfloat16 [65536, 4096], P(('dp', 'head')), may hold values from -6 to 6
- key_rows: bfloat16 [65536, 1024], P(('dp', 'head')), may hold values from -6 to 6
- values: bfloat16 [65536, 1024], P(('dp', 'head')), may hold values from -6 to 6
- cotangent: bfloat16 [65536, 4096], P(('dp', 'head')), may hold values from -6 to 6
- block_route: int32 [512, 2], replicated, may hold values from 0 to 63, as said below
- doc_start: int32 [512], replicated, may hold values from 0 to 65408, as said below
Outputs:
- grad_queries: bfloat16 [65536, 4096], P('dp', 'head')
- grad_keys: bfloat16 [65536, 1024], P('dp', 'head')
- grad_values: bfloat16 [65536, 1024], P('dp', 'head')
Inputs may be any that keep to these rules, and one draw needn't show every extreme that they name: `block_route`: row b gives the dp index and the slot, among that index's 8 slots, of block b in the attention placement. The dp indices 2p and 2p + 1 are partners: each hands exactly half of its aligned bins of 4 blocks, whole, to the other, into the slots of the bins that the other hands over, in order; every other block keeps its dp index and slot. After the move no dp index holds more than 16 pairs of a query block and a key block at or before it in the same document. `doc_start`: each entry is the first token of its block's document; documents are runs of whole blocks inside aligned bins of 4 blocks.
All inputs are finite; a program needn't handle non-finite values.
Results may differ from a plain program's by a relative error of at most 0.023.
Values may be sent and summed in bfloat16 or wider, within the bound.
A program may use at most 64 MiB of HBM per device.

v0:
```python
import jax
import jax.numpy as jnp
import numpy as np
from jax import lax
from jax.sharding import PartitionSpec as P

HEAD_DIM = 128
BLOCK = 128


def swapped(x, axis, stride):
    return lax.ppermute(x, axis, [(i, i ^ 1 << stride) for i in range(lax.axis_size(axis))])


def pair_tables(blocks_dev):
    query_list = []
    key_list = []
    for bin_first in range(0, blocks_dev, 4):
        for query_off in range(4):
            for key_off in range(query_off + 1):
                query_list.append(bin_first + query_off)
                key_list.append(bin_first + key_off)
    return (np.array(query_list, dtype=np.int32), np.array(key_list, dtype=np.int32))


def outgoing_plan(route_part, dp_index, blocks_dev):
    slot_index = jnp.arange(blocks_dev, dtype=jnp.int32)
    moved_out = route_part[:, 0] != dp_index
    sort_keys = jnp.where(moved_out, route_part[:, 1], blocks_dev + slot_index)
    return (moved_out, jnp.argsort(sort_keys, stable=True)[: blocks_dev // 2])


def settle(local, arriving, vacated):
    half_count = arriving.shape[0]
    slot_rank = jnp.clip(jnp.cumsum(vacated.astype(jnp.int32)) - 1, 0, half_count - 1)
    pulled = jnp.take(arriving, slot_rank, axis=0)
    slot_mask = vacated.reshape((-1,) + (1,) * (local.ndim - 1))
    return jnp.where(slot_mask, pulled, local)


def attend(q_blocks, k_blocks, v_blocks, d_blocks, doc_slots, tile_cap):
    blocks_dev = q_blocks.shape[0]
    block_len = q_blocks.shape[1]
    query_heads = q_blocks.shape[2] // HEAD_DIM
    value_heads = k_blocks.shape[2] // HEAD_DIM
    per_group = query_heads // value_heads
    softmax_scale = HEAD_DIM ** (-0.5)
    highest = lax.Precision.HIGHEST
    query_table, key_table = pair_tables(blocks_dev)
    query_side = jnp.asarray(query_table)
    key_side = jnp.asarray(key_table)
    live_pair = jnp.take(doc_slots, query_side) == jnp.take(doc_slots, key_side)
    chosen = jnp.argsort(jnp.where(live_pair, 0, 1), stable=True)[:tile_cap]
    query_side = jnp.take(query_side, chosen)
    key_side = jnp.take(key_side, chosen)
    live_pair = jnp.take(live_pair, chosen)
    q_slots = q_blocks.reshape(blocks_dev, block_len, value_heads, per_group, HEAD_DIM)
    d_slots = d_blocks.reshape(blocks_dev, block_len, value_heads, per_group, HEAD_DIM)
    q_tiles = jnp.take(q_slots, query_side, axis=0)
    d_tiles = jnp.take(d_slots, query_side, axis=0)
    k_tiles = jnp.take(
        k_blocks.reshape(blocks_dev, block_len, value_heads, HEAD_DIM), key_side, axis=0
    )
    v_tiles = jnp.take(
        v_blocks.reshape(blocks_dev, block_len, value_heads, HEAD_DIM), key_side, axis=0
    )
    row_index = jnp.arange(block_len)
    causal = row_index[None, :] <= row_index[:, None]
    allowed = live_pair[:, None, None] & ((query_side != key_side)[:, None, None] | causal[None])
    scores = (
        jnp.einsum("tqcgd,tkcd->tcgqk", q_tiles, k_tiles, preferred_element_type=jnp.float32)
        * softmax_scale
    )
    scores = jnp.where(allowed[:, None, None], scores, -jnp.inf)
    slot_ids = jnp.arange(blocks_dev, dtype=jnp.int32)
    query_onehot = query_side[:, None] == slot_ids[None, :]
    tile_top = jnp.max(scores, axis=-1)
    slot_top = jnp.max(
        jnp.where(query_onehot.T[:, :, None, None, None], tile_top[None], -jnp.inf), axis=1
    )
    exp_scores = jnp.exp(scores - jnp.take(slot_top, query_side, axis=0)[..., None])
    query_mix = query_onehot.astype(jnp.float32)
    key_mix = (key_side[:, None] == slot_ids[None, :]).astype(jnp.float32)
    slot_total = jnp.einsum(
        "ts,tcgq->scgq", query_mix, jnp.sum(exp_scores, axis=-1), precision=highest
    )
    weights = lax.optimization_barrier(
        (exp_scores / jnp.take(slot_total, query_side, axis=0)[..., None]).astype(jnp.bfloat16)
    )
    attended_tiles = jnp.einsum(
        "tcgqk,tkcd->tqcgd", weights, v_tiles, preferred_element_type=jnp.float32
    )
    attended = jnp.einsum("ts,tqcgd->sqcgd", query_mix, attended_tiles, precision=highest).astype(
        jnp.bfloat16
    )
    row_delta = jnp.sum(d_slots.astype(jnp.float32) * attended.astype(jnp.float32), axis=-1)
    tile_delta = jnp.transpose(jnp.take(row_delta, query_side, axis=0), (0, 2, 3, 1))
    dweights = jnp.einsum("tqcgd,tkcd->tcgqk", d_tiles, v_tiles, preferred_element_type=jnp.float32)
    dscores = lax.optimization_barrier(
        (weights.astype(jnp.float32) * (dweights - tile_delta[..., None])).astype(jnp.bfloat16)
    )
    grad_q_tiles = jnp.einsum(
        "tcgqk,tkcd->tqcgd", dscores, k_tiles, preferred_element_type=jnp.float32
    )
    grad_k_tiles = jnp.einsum(
        "tcgqk,tqcgd->tkcd", dscores, q_tiles, preferred_element_type=jnp.float32
    )
    grad_v_tiles = jnp.einsum(
        "tcgqk,tqcgd->tkcd", weights, d_tiles, preferred_element_type=jnp.float32
    )
    grad_q = (
        softmax_scale * jnp.einsum("ts,tqcgd->sqcgd", query_mix, grad_q_tiles, precision=highest)
    ).astype(jnp.bfloat16)
    grad_k = (
        softmax_scale * jnp.einsum("ts,tkcd->skcd", key_mix, grad_k_tiles, precision=highest)
    ).astype(jnp.bfloat16)
    grad_v = jnp.einsum("ts,tkcd->skcd", key_mix, grad_v_tiles, precision=highest).astype(
        jnp.bfloat16
    )
    return (
        grad_q.reshape(blocks_dev, block_len, query_heads * HEAD_DIM),
        grad_k.reshape(blocks_dev, block_len, value_heads * HEAD_DIM),
        grad_v.reshape(blocks_dev, block_len, value_heads * HEAD_DIM),
    )


def body(queries, key_rows, values, cotangent, block_route, doc_start):
    q_group, k_group, v_group, d_group = (
        lax.all_to_all(queries, "head", split_axis=1, concat_axis=0, tiled=True),
        lax.all_to_all(key_rows, "head", split_axis=1, concat_axis=0, tiled=True),
        lax.all_to_all(values, "head", split_axis=1, concat_axis=0, tiled=True),
        lax.all_to_all(cotangent, "head", split_axis=1, concat_axis=0, tiled=True),
    )
    blocks_dev = q_group.shape[0] // BLOCK

    def blocked(tensor):
        return tensor.reshape(blocks_dev, BLOCK, tensor.shape[1])

    q_blocks = blocked(q_group)
    k_blocks = blocked(k_group)
    v_blocks = blocked(v_group)
    d_blocks = blocked(d_group)
    own_dp = lax.axis_index("dp")
    partner = jnp.bitwise_xor(own_dp, 1)
    route_own = lax.dynamic_slice_in_dim(block_route, own_dp * blocks_dev, blocks_dev, 0)
    route_mate = lax.dynamic_slice_in_dim(block_route, partner * blocks_dev, blocks_dev, 0)
    slot_index = jnp.arange(blocks_dev, dtype=jnp.int32)
    moved_out, send_order = outgoing_plan(route_own, own_dp, blocks_dev)
    mate_order = outgoing_plan(route_mate, partner, blocks_dev)[1]
    own_ids = own_dp * blocks_dev + slot_index
    settled_ids = settle(own_ids, partner * blocks_dev + mate_order, moved_out)
    arrived_q, arrived_k, arrived_v, arrived_d = swapped(
        (
            jnp.take(q_blocks, send_order, axis=0),
            jnp.take(k_blocks, send_order, axis=0),
            jnp.take(v_blocks, send_order, axis=0),
            jnp.take(d_blocks, send_order, axis=0),
        ),
        "dp",
        0,
    )
    grad_q, grad_k, grad_v = attend(
        settle(q_blocks, arrived_q, moved_out),
        settle(k_blocks, arrived_k, moved_out),
        settle(v_blocks, arrived_v, moved_out),
        settle(d_blocks, arrived_d, moved_out),
        jnp.take(doc_start, settled_ids),
        2 * blocks_dev,
    )
    rows = blocks_dev * BLOCK
    return (
        grad_q.reshape(rows, grad_q.shape[2]),
        grad_k.reshape(rows, grad_k.shape[2]),
        grad_v.reshape(rows, grad_v.shape[2]),
    )


def solution(mesh):
    placed = (
        P(("dp", "head"), None),
        P(("dp", "head"), None),
        P(("dp", "head"), None),
        P(("dp", "head"), None),
        P(),
        P(),
    )
    return jax.shard_map(
        body,
        mesh=mesh,
        in_specs=placed,
        out_specs=(P("dp", "head"), P("dp", "head"), P("dp", "head")),
        check_vma=False,
    )
```

profile of v0, /device:TPU:1, one launch (start us, length us, event | category | flops | bytes accessed | tf_op | source)
XLA Modules:
  0.0 181.8 jit_solution(9863108649951106653)
XLA Ops:
  0.7 1.2 copy.134
  1.9 0.9 copy.135
  2.7 10.3 %all-to-all-start = ((bf16[128,8,128]{2,0,1:T(8,128)(2,1)}), bf16[128,8,128]{2,0,1:T(8,128)(2,1)S(1)}, u32[]{:S(2)}, u32[]{:S(2)}) async-start(bf16[128,8,128]{2,0,1:T(8,128)(2,1)} %copy.135), calls=%async_computation | async-start | bytes 524288 | tf_op jit(solution)/shard_map/all_to_all | solution.py:130
  13.0 0.8 constant_dynamic-slice_fusion
  14.1 1.0 sort.48
  15.7 0.6 gather_fusion.1
  16.4 0.7 gather_fusion.4
  17.1 0.7 gather_fusion.5
  18.0 0.9 copy.143
  18.9 1.6 sort.49
  20.5 4.8 %all-to-all-start.2 = ((bf16[128,8,128]{2,0,1:T(8,128)(2,1)}), bf16[128,8,128]{2,0,1:T(8,128)(2,1)S(1)}, u32[]{:S(2)}, u32[]{:S(2)}) async-start(bf16[128,8,128]{2,0,1:T(8,128)(2,1)} %copy.143), calls=%async_computation.2 | async-start | bytes 524288 | tf_op jit(solution)/shard_map/all_to_all | solution.py:131
  25.4 0.7 copy.136
  26.0 1.3 copy.137
  27.4 1.0 sort.50
  28.8 3.0 %all-to-all-done.2 = bf16[128,8,128]{2,0,1:T(8,128)(2,1)S(1)} async-done(((bf16[128,8,128]{2,0,1:T(8,128)(2,1)}), bf16[128,8,128]{2,0,1:T(8,128)(2,1)S(1)}, u32[]{:S(2)}, u32[]{:S(2)}) %all-to-all-start.2) | async-done | bytes 262176 | tf_op jit(solution)/shard_map/all_to_all | solution.py:131
  31.9 0.7 copy-done.12
  32.6 4.5 %all-to-all-start.1 = ((bf16[128,8,512]{2,0,1:T(8,128)(2,1)}), bf16[128,8,512]{2,0,1:T(8,128)(2,1)S(1)}, u32[]{:S(2)}, u32[]{:S(2)}) async-start(bf16[128,8,512]{2,0,1:T(8,128)(2,1)} %copy.137), calls=%async_computation.1 | async-start | bytes 2097152 | tf_op jit(solution)/shard_map/all_to_all | solution.py:129
  37.1 0.7 gather_fusion.6
  37.7 0.7 gather_fusion.9
  38.4 0.7 copy.144
  39.1 1.3 copy.145
  40.4 0.7 gather_fusion.2
  42.2 10.0 %all-to-all-done.1 = bf16[128,8,512]{2,0,1:T(8,128)(2,1)S(1)} async-done(((bf16[128,8,512]{2,0,1:T(8,128)(2,1)}), bf16[128,8,512]{2,0,1:T(8,128)(2,1)S(1)}, u32[]{:S(2)}, u32[]{:S(2)}) %all-to-all-start.1) | async-done | bytes 1048608 | tf_op jit(solution)/shard_map/all_to_all | solution.py:129
  52.2 4.3 %all-to-all-start.3 = ((bf16[128,8,512]{2,0,1:T(8,128)(2,1)}), bf16[128,8,512]{2,0,1:T(8,128)(2,1)S(1)}, u32[]{:S(2)}, u32[]{:S(2)}) async-start(bf16[128,8,512]{2,0,1:T(8,128)(2,1)} %copy.145), calls=%async_computation.3 | async-start | bytes 2097152 | tf_op jit(solution)/shard_map/all_to_all | solution.py:132
  59.0 1.2 gather_fusion.16
  60.8 10.8 %all-to-all-done.3 = bf16[128,8,512]{2,0,1:T(8,128)(2,1)S(1)} async-done(((bf16[128,8,512]{2,0,1:T(8,128)(2,1)}), bf16[128,8,512]{2,0,1:T(8,128)(2,1)S(1)}, u32[]{:S(2)}, u32[]{:S(2)}) %all-to-all-start.3) | async-done | bytes 1048608 | tf_op jit(solution)/shard_map/all_to_all | solution.py:132
  72.2 1.8 broadcast_select_fusion
  74.0 1.9 %collective-permute-start.1 = (bf16[4,128,512]{2,1,0:T(8,128)(2,1)}, bf16[4,128,512]{2,1,0:T(8,128)(2,1)}, u32[]{:S(2)}, u32[]{:S(2)}) collective-permute-start(bf16[4,128,512]{2,1,0:T(8,128)(2,1)} %get-tuple-element.53), channel_id=1, source_target_pairs={{0,8},{8,0},{16,24},{24,16},{32,40},{40,32},{48,56},{56,48},{64,72... | collective-permute-start | bytes 1572872 | tf_op jit(solution)/shard_map/ppermute | solution.py:12
  75.9 3.4 %collective-permute-start.3 = (bf16[4,128,512]{2,1,0:T(8,128)(2,1)}, bf16[4,128,512]{2,1,0:T(8,128)(2,1)S(1)}, u32[]{:S(2)}, u32[]{:S(2)}) collective-permute-start(bf16[4,128,512]{2,1,0:T(8,128)(2,1)} %get-tuple-element.52), channel_id=1, source_target_pairs={{0,8},{8,0},{16,24},{24,16},{32,40},{40,32},{48,56},{56,48},{64,72... | collective-permute-start | bytes 1572872 | tf_op jit(solution)/shard_map/ppermute | solution.py:12
  79.3 0.7 broadcast_select_fusion.2
  80.0 1.9 %collective-permute-start = (bf16[4,128,128]{2,1,0:T(8,128)(2,1)S(1)}, bf16[4,128,128]{2,1,0:T(8,128)(2,1)S(1)}, u32[]{:S(2)}, u32[]{:S(2)}) collective-permute-start(bf16[4,128,128]{2,1,0:T(8,128)(2,1)S(1)} %get-tuple-element.51), channel_id=1, source_target_pairs={{0,8},{8,0},{16,24},{24,16},{32,40},{40,32},{48,56},{56,48},{64,72... | collective-permute-start | bytes 393224 | tf_op jit(solution)/shard_map/ppermute | solution.py:12
  81.9 3.4 %collective-permute-start.2 = (bf16[4,128,128]{2,1,0:T(8,128)(2,1)S(1)}, bf16[4,128,128]{2,1,0:T(8,128)(2,1)S(1)}, u32[]{:S(2)}, u32[]{:S(2)}) collective-permute-start(bf16[4,128,128]{2,1,0:T(8,128)(2,1)S(1)} %get-tuple-element.50), channel_id=1, source_target_pairs={{0,8},{8,0},{16,24},{24,16},{32,40},{40,32},{48,56},{56,48},{64,72... | collective-permute-start | bytes 393224 | tf_op jit(solution)/shard_map/ppermute | solution.py:12
  86.5 16.2 %collective-permute-done = bf16[4,128,128]{2,1,0:T(8,128)(2,1)S(1)} collective-permute-done((bf16[4,128,128]{2,1,0:T(8,128)(2,1)S(1)}, bf16[4,128,128]{2,1,0:T(8,128)(2,1)S(1)}, u32[]{:S(2)}, u32[]{:S(2)}) %collective-permute-start) | collective-permute-done | bytes 131104 | tf_op jit(solution)/shard_map/ppermute | solution.py:12
  102.7 1.3 gather_fusion.8
  104.0 1.5 collective-permute-done.2
  105.5 1.3 gather_fusion.17
  106.8 1.3 select_select_fusion.2
  108.1 1.4 gather_fusion.10
  109.5 1.4 gather_fusion.18
  111.0 2.6 %gather_fusion.12 = bf16[8,128,512]{2,1,0:T(8,128)(2,1)} fusion(bf16[4,128,512]{2,1,0:T(8,128)(2,1)} %collective-permute-done.1, s32[1024]{0:T(1024)S(1)} %pad_clamp_fusion.2), kind=kCustom, calls=%fused_computation.6.clone | custom fusion | bytes 2097184 | tf_op jit(solution)/shard_map/jit(_take)/gather | solution.py:36
  113.6 1.6 gather_fusion.20
  115.2 3.0 %select_select_fusion = (bf16[8,128,512]{2,1,0:T(8,128)(2,1)S(1)}, bf16[8,128,512]{2,1,0:T(8,128)(2,1)}) fusion(bf16[8,128,512]{2,1,0:T(8,128)(2,1)} %gather_fusion.20, pred[8]{0:T(512)(128)(4,1)S(1)} %copy-done.24, pred[8]{0:T(512)(128)(4,1)S(1)} %bitcast.241, bf16[128,8,512]{2,0,1:T(8,128)(2,1)S(1)} %all-to-all-done.3, ...), kind=kLoop, calls=%fused_computation.56 | loop fusion | flops 2097152 | bytes 6291472 | tf_op jit(solution)/shard_map/jit(_where)/select_n | solution.py:38
  118.1 1.6 copy.147
  119.8 1.2 reshape.331
  121.5 1.0 gather_fusion.13
  122.5 4.6 %fusion.3 = (f32[16,4,128]{2,1,0:T(4,128)S(1)}, f32[16,128,128,4]{2,1,3,0:T(8,128)}) fusion(pred[16,128,128]{1,2,0:T(8,128)(4,1)S(1)} %or_and_fusion, bf16[16,128,4,128]{3,1,2,0:T(8,128)(2,1)S(1)} %gather_fusion.13, pred[16]{0:T(512)(128)(4,1)S(1)} %get-tuple-element.57, bf16[16,128,128]{2,1,0:T(8,128)(2,1)} %gather_fusion.10, pred[16]{0:T(512)(128)(4,1)S(1)} %copy-done.23), kind=kOutput, calls=%fused_computation.29 | convolution fusion | flops 272883712 | bytes 7110688 | tf_op jit(solution)/shard_map/tqcgd,tkcd->tcgqk/dot_general | solution.py:71
  127.9 3.3 %fusion.2 = f32[16,4,128]{2,1,0:T(4,128)S(1)} fusion(f32[16,128,128,4]{2,1,3,0:T(8,128)} %get-tuple-element.56, f32[16,4,128]{2,1,0:T(4,128)S(1)} %fusion.32, pred[16,128,128]{1,2,0:T(8,128)(4,1)S(1)} %or_and_fusion), kind=kLoop, calls=%fused_computation.28 | loop fusion | flops 4186112 | bytes 4521984 | tf_op jit(solution)/shard_map/reduce_sum | solution.py:85
  132.1 3.6 %divide_convert_fusion = bf16[16,1,4,128,128]{3,4,2,0,1:T(8,128)(2,1)S(1)} fusion(f32[16,128,128,4]{2,1,3,0:T(8,128)} %get-tuple-element.56, f32[16,4,128]{2,1,0:T(4,128)S(1)} %fusion.31, f32[16,4,128]{2,1,0:T(4,128)S(1)} %fusion.32, pred[16,128,128]{1,2,0:T(8,128)(4,1)S(1)} %or_and_fusion), kind=kLoop, calls=%fused_computation.26 | loop fusion | flops 5242880 | bytes 6619136 | tf_op jit(solution)/shard_map/convert_element_type | solution.py:88
  135.6 2.9 %convolution_bitcast_fusion.1 = f32[16,128,4,128]{1,3,2,0:T(8,128)} fusion(bf16[16,1,4,128,128]{3,4,2,0,1:T(8,128)(2,1)S(1)} %divide_convert_fusion, bf16[16,128,128]{2,1,0:T(8,128)(2,1)S(1)} %copy-done.9, pred[16]{0:T(512)(128)(4,1)S(1)} %copy-done.23), kind=kOutput, calls=%fused_computation.31 | convolution fusion | flops 268697600 | bytes 6815760 | tf_op jit(solution)/shard_map/tcgqk,tkcd->tqcgd/dot_general | solution.py:90
  138.5 5.5 %copy.150 = f32[16,128,4,128]{3,0,2,1:T(8,128)} copy(f32[16,128,4,128]{1,3,2,0:T(8,128)} %convolution_bitcast_fusion.1) | data formatting | bytes 8388608 | tf_op jit(solution)/shard_map/reshape.50
  144.0 3.1 %copy.151 = f32[8,128,4,128]{3,0,2,1:T(8,128)} copy(f32[8,128,4,128]{1,3,2,0:T(8,128)} %bitcast.227) | data formatting | bytes 4194304 | tf_op jit(solution)/shard_map/convert_element_type | solution.py:96
  147.2 4.9 %multiply_reduce_fusion = f32[8,128,4]{0,2,1:T(4,128)S(1)} fusion(f32[8,128,4,128]{3,0,2,1:T(8,128)} %copy.151, f32[16,128,4,128]{3,0,2,1:T(8,128)} %copy.150, s32[16]{0:T(128)S(1)} %get-tuple-element.35), kind=kOutput, calls=%fused_computation.46 | convolution fusion | flops 102756480 | bytes 6307904 | tf_op jit(solution)/shard_map/ts,tqcgd->sqcgd/dot_general | solution.py:93
  152.8 1.5 copy.192
  154.3 2.1 %gather_fusion.21 = bf16[16,128,4,128]{3,1,2,0:T(8,128)(2,1)} fusion(bf16[8,128,4,128]{3,1,2,0:T(8,128)(2,1)S(1)} %bitcast.225, s32[1024]{0:T(1024)S(1)} %pad_clamp_fusion), kind=kCustom, calls=%fused_computation.16.clone | custom fusion | bytes 4194368 | tf_op jit(solution)/shard_map/jit(_take)/gather | solution.py:60
  156.5 3.1 %fusion.1 = bf16[16,1,4,128,128]{3,4,2,0,1:T(8,128)(2,1)S(1)} fusion(bf16[16,1,4,128,128]{3,4,2,0,1:T(8,128)(2,1)S(1)} %divide_convert_fusion, f32[16,4,128]{2,1,0:T(4,128)S(1)} %fusion.30, bf16[16,128,4,128]{3,1,2,0:T(8,128)(2,1)} %gather_fusion.21, pred[16]{0:T(512)(128)(4,1)S(1)} %get-tuple-element.57, bf16[16,128,128]{2,1,0:T(8,128)(2,1)} %gather_fusion.18, ...), kind=kOutput, calls=%fused_computation.24 | convolution fusion | flops 273940480 | bytes 6848544 | tf_op jit(solution)/shard_map/tqcgd,tkcd->tcgqk/dot_general | solution.py:98
  159.6 1.8 fusion.20
  161.4 2.9 %convolution_bitcast_fusion = f32[16,128,4,128]{1,3,2,0:T(8,128)} fusion(bf16[16,1,4,128,128]{3,4,2,0,1:T(8,128)(2,1)S(1)} %fusion.1, bf16[16,128,128]{2,1,0:T(8,128)(2,1)S(1)} %copy-done.8, pred[16]{0:T(512)(128)(4,1)S(1)} %copy-done.23), kind=kOutput, calls=%fused_computation.30 | convolution fusion | flops 268697600 | bytes 6815760 | tf_op jit(solution)/shard_map/tcgqk,tkcd->tqcgd/dot_general | solution.py:102
  164.3 1.9 %fusion.15 = f32[16,128,128]{1,2,0:T(8,128)} fusion(bf16[16,1,4,128,128]{3,4,2,0,1:T(8,128)(2,1)S(1)} %divide_convert_fusion, bf16[16,128,4,128]{3,1,2,0:T(8,128)(2,1)S(1)} %copy-done.7, pred[16]{0:T(512)(128)(4,1)S(1)} %get-tuple-element.57), kind=kOutput, calls=%fused_computation.48 | convolution fusion | flops 269484032 | bytes 5242896 | tf_op jit(solution)/shard_map/tcgqk,tqcgd->tkcd/dot_general | solution.py:108
  166.2 1.7 copy.159
  168.4 0.7 copy.160
  169.1 5.5 %copy.155 = f32[16,128,4,128]{3,0,2,1:T(8,128)} copy(f32[16,128,4,128]{1,3,2,0:T(8,128)} %convolution_bitcast_fusion) | data formatting | bytes 8388608 | tf_op jit(solution)/shard_map/reshape.56
  174.6 3.9 %multiply_convert_fusion = bf16[8,128,4,128]{3,0,2,1:T(8,128)(2,1)S(1)} fusion(f32[16,128,4,128]{3,0,2,1:T(8,128)} %copy.155, s32[16]{0:T(128)S(1)} %get-tuple-element.35), kind=kOutput, calls=%fused_computation.45 | convolution fusion | flops 101712000 | bytes 5242944 | tf_op jit(solution)/shard_map/ts,tqcgd->sqcgd/dot_general | solution.py:112
  179.0 1.2 copy.191
  181.1 0.7 copy.164
  (107 shorter events, 12.5 us)
Async XLA Ops:
  0.6 15.1 %copy-start = (s32[512]{0:T(512)S(1)}, s32[512]{0:T(512)}, u32[]{:S(2)}) copy-start(s32[512]{0:T(512)} %param.31) | copy-start | bytes 6148
  0.6 15.7 %copy-start.3 = (s32[20]{0:T(128)S(1)}, s32[20]{0:T(128)}, u32[]{:S(2)}) copy-start(s32[20]{0:T(128)} %constant.209) | copy-start | bytes 244
  0.7 15.8 %copy-start.2 = (s32[20]{0:T(128)S(1)}, s32[20]{0:T(128)}, u32[]{:S(2)}) copy-start(s32[20]{0:T(128)} %constant.210) | copy-start | bytes 244
  0.7 17.2 %copy-start.18 = (bf16[128,1024]{1,0:T(8,128)(2,1)S(1)}, bf16[128,1024]{1,0:T(8,128)(2,1)}, u32[]{:S(2)}) copy-start(bf16[128,1024]{1,0:T(8,128)(2,1)} %param.28) | copy-start | bytes 786436
  2.7 22.7 %copy-start.14 = (bf16[128,4096]{1,0:T(8,128)(2,1)S(1)}, bf16[128,4096]{1,0:T(8,128)(2,1)}, u32[]{:S(2)}) copy-start(bf16[128,4096]{1,0:T(8,128)(2,1)} %param.26) | copy-start | bytes 3145732
  2.7 17.8 %all-to-all-start = ((bf16[128,8,128]{2,0,1:T(8,128)(2,1)}), bf16[128,8,128]{2,0,1:T(8,128)(2,1)S(1)}, u32[]{:S(2)}, u32[]{:S(2)}) async-start(bf16[128,8,128]{2,0,1:T(8,128)(2,1)} %copy.135), calls=%async_computation | async-start | bytes 524288 | tf_op jit(solution)/shard_map/all_to_all | solution.py:130
  13.9 11.5 %copy-start.21 = (pred[8,1]{0,1:T(4,128)(4,1)}, pred[8,1]{0,1:T(4,128)(4,1)S(1)}, u32[]{:S(2)}) copy-start(pred[8,1]{0,1:T(4,128)(4,1)S(1)} %get-tuple-element.41) | copy-start | bytes 28
  20.5 4.8 %copy-start.10 = (bf16[128,8,128]{2,0,1:T(8,128)(2,1)}, bf16[128,8,128]{2,0,1:T(8,128)(2,1)S(1)}, u32[]{:S(2)}) copy-start(bf16[128,8,128]{2,0,1:T(8,128)(2,1)S(1)} %all-to-all-done) | copy-start | bytes 786436
  20.5 11.3 %all-to-all-start.2 = ((bf16[128,8,128]{2,0,1:T(8,128)(2,1)}), bf16[128,8,128]{2,0,1:T(8,128)(2,1)S(1)}, u32[]{:S(2)}, u32[]{:S(2)}) async-start(bf16[128,8,128]{2,0,1:T(8,128)(2,1)} %copy.143), calls=%async_computation.2 | async-start | bytes 524288 | tf_op jit(solution)/shard_map/all_to_all | solution.py:131
  27.4 11.0 %copy-start.15 = (bf16[128,4096]{1,0:T(8,128)(2,1)S(1)}, bf16[128,4096]{1,0:T(8,128)(2,1)}, u32[]{:S(2)}) copy-start(bf16[128,4096]{1,0:T(8,128)(2,1)} %param.29) | copy-start | bytes 3145732
  31.9 0.7 copy-start.12
  32.6 19.6 %all-to-all-start.1 = ((bf16[128,8,512]{2,0,1:T(8,128)(2,1)}), bf16[128,8,512]{2,0,1:T(8,128)(2,1)S(1)}, u32[]{:S(2)}, u32[]{:S(2)}) async-start(bf16[128,8,512]{2,0,1:T(8,128)(2,1)} %copy.137), calls=%async_computation.1 | async-start | bytes 2097152 | tf_op jit(solution)/shard_map/all_to_all | solution.py:129
  40.4 18.1 %copy-start.11 = (bf16[128,8,128]{2,0,1:T(8,128)(2,1)S(1)}, bf16[128,8,128]{2,0,1:T(8,128)(2,1)}, u32[]{:S(2)}) copy-start(bf16[128,8,128]{2,0,1:T(8,128)(2,1)} %copy-done.10) | copy-start | bytes 786436
  40.4 18.6 %copy-start.13 = (bf16[128,8,128]{2,0,1:T(8,128)(2,1)S(1)}, bf16[128,8,128]{2,0,1:T(8,128)(2,1)}, u32[]{:S(2)}) copy-start(bf16[128,8,128]{2,0,1:T(8,128)(2,1)} %copy-done.12) | copy-start | bytes 786436
  41.1 17.1 %copy-start.19 = (s32[16]{0:T(128)}, s32[16]{0:T(128)S(1)}, u32[]{:S(2)}) copy-start(s32[16]{0:T(128)S(1)} %get-tuple-element.34) | copy-start | bytes 196
  52.2 19.5 %all-to-all-start.3 = ((bf16[128,8,512]{2,0,1:T(8,128)(2,1)}), bf16[128,8,512]{2,0,1:T(8,128)(2,1)S(1)}, u32[]{:S(2)}, u32[]{:S(2)}) async-start(bf16[128,8,512]{2,0,1:T(8,128)(2,1)} %copy.145), calls=%async_computation.3 | async-start | bytes 2097152 | tf_op jit(solution)/shard_map/all_to_all | solution.py:132
  72.2 7.1 %copy-start.17 = (bf16[4,128,128]{2,1,0:T(8,128)(2,1)S(1)}, bf16[4,128,128]{2,1,0:T(8,128)(2,1)}, u32[]{:S(2)}) copy-start(bf16[4,128,128]{2,1,0:T(8,128)(2,1)} %gather_fusion.16) | copy-start | bytes 393220
  72.2 34.6 %copy-start.22 = (pred[8,1]{0,1:T(4,128)(4,1)S(1)}, pred[8,1]{0,1:T(4,128)(4,1)}, u32[]{:S(2)}) copy-start(pred[8,1]{0,1:T(4,128)(4,1)} %copy-done.21) | copy-start | bytes 28
  74.0 37.0 %collective-permute-start.1 = (bf16[4,128,512]{2,1,0:T(8,128)(2,1)}, bf16[4,128,512]{2,1,0:T(8,128)(2,1)}, u32[]{:S(2)}, u32[]{:S(2)}) collective-permute-start(bf16[4,128,512]{2,1,0:T(8,128)(2,1)} %get-tuple-element.53), channel_id=1, source_target_pairs={{0,8},{8,0},{16,24},{24,16},{32,40},{40,32},{48,56},{56,48},{64,72... | collective-permute-start | bytes 1572872 | tf_op jit(solution)/shard_map/ppermute | solution.py:12
  75.9 37.7 %collective-permute-start.3 = (bf16[4,128,512]{2,1,0:T(8,128)(2,1)}, bf16[4,128,512]{2,1,0:T(8,128)(2,1)S(1)}, u32[]{:S(2)}, u32[]{:S(2)}) collective-permute-start(bf16[4,128,512]{2,1,0:T(8,128)(2,1)} %get-tuple-element.52), channel_id=1, source_target_pairs={{0,8},{8,0},{16,24},{24,16},{32,40},{40,32},{48,56},{56,48},{64,72... | collective-permute-start | bytes 1572872 | tf_op jit(solution)/shard_map/ppermute | solution.py:12
  80.0 22.7 %collective-permute-start = (bf16[4,128,128]{2,1,0:T(8,128)(2,1)S(1)}, bf16[4,128,128]{2,1,0:T(8,128)(2,1)S(1)}, u32[]{:S(2)}, u32[]{:S(2)}) collective-permute-start(bf16[4,128,128]{2,1,0:T(8,128)(2,1)S(1)} %get-tuple-element.51), channel_id=1, source_target_pairs={{0,8},{8,0},{16,24},{24,16},{32,40},{40,32},{48,56},{56,48},{64,72... | collective-permute-start | bytes 393224 | tf_op jit(solution)/shard_map/ppermute | solution.py:12
  81.9 23.6 %collective-permute-start.2 = (bf16[4,128,128]{2,1,0:T(8,128)(2,1)S(1)}, bf16[4,128,128]{2,1,0:T(8,128)(2,1)S(1)}, u32[]{:S(2)}, u32[]{:S(2)}) collective-permute-start(bf16[4,128,128]{2,1,0:T(8,128)(2,1)S(1)} %get-tuple-element.50), channel_id=1, source_target_pairs={{0,8},{8,0},{16,24},{24,16},{32,40},{40,32},{48,56},{56,48},{64,72... | collective-permute-start | bytes 393224 | tf_op jit(solution)/shard_map/ppermute | solution.py:12
  111.0 4.2 %copy-start.24 = (pred[8]{0:T(512)(128)(4,1)S(1)}, pred[8]{0:T(512)(128)(4,1)}, u32[]{:S(2)}) copy-start(pred[8]{0:T(512)(128)(4,1)} %get-tuple-element.38) | copy-start | bytes 28
  118.1 2.8 %copy-start.4 = (bf16[8,128,512]{2,1,0:T(8,128)(2,1)S(1)}, bf16[8,128,512]{2,1,0:T(8,128)(2,1)}, u32[]{:S(2)}) copy-start(bf16[8,128,512]{2,1,0:T(8,128)(2,1)} %get-tuple-element.49) | copy-start | bytes 3145732
  121.5 1.0 copy-start.23
  122.4 4.6 %copy-start.5 = (bf16[16,128,4,128]{3,1,2,0:T(8,128)(2,1)}, bf16[16,128,4,128]{3,1,2,0:T(8,128)(2,1)S(1)}, u32[]{:S(2)}) copy-start(bf16[16,128,4,128]{3,1,2,0:T(8,128)(2,1)S(1)} %gather_fusion.13) | copy-start | bytes 6291460
  122.4 4.6 %copy-start.25 = (pred[8,16]{1,0:T(8,128)(4,1)S(1)}, pred[8,16]{1,0:T(8,128)(4,1)}, u32[]{:S(2)}) copy-start(pred[8,16]{1,0:T(8,128)(4,1)} %iota_compare_fusion.2) | copy-start | bytes 388
  132.1 3.6 %copy-start.9 = (bf16[16,128,128]{2,1,0:T(8,128)(2,1)S(1)}, bf16[16,128,128]{2,1,0:T(8,128)(2,1)}, u32[]{:S(2)}) copy-start(bf16[16,128,128]{2,1,0:T(8,128)(2,1)} %gather_fusion.18) | copy-start | bytes 1572868
  156.5 3.1 %copy-start.6 = (bf16[16,128,4,128]{3,1,2,0:T(8,128)(2,1)S(1)}, bf16[16,128,4,128]{3,1,2,0:T(8,128)(2,1)}, u32[]{:S(2)}) copy-start(bf16[16,128,4,128]{3,1,2,0:T(8,128)(2,1)} %copy-done.5) | copy-start | bytes 6291460
  159.6 1.8 %copy-start.8 = (bf16[16,128,128]{2,1,0:T(8,128)(2,1)S(1)}, bf16[16,128,128]{2,1,0:T(8,128)(2,1)}, u32[]{:S(2)}) copy-start(bf16[16,128,128]{2,1,0:T(8,128)(2,1)} %gather_fusion.10) | copy-start | bytes 1572868
  161.4 2.9 %copy-start.7 = (bf16[16,128,4,128]{3,1,2,0:T(8,128)(2,1)S(1)}, bf16[16,128,4,128]{3,1,2,0:T(8,128)(2,1)}, u32[]{:S(2)}) copy-start(bf16[16,128,4,128]{3,1,2,0:T(8,128)(2,1)} %gather_fusion.21) | copy-start | bytes 6291460
  166.2 1.7 copy-start.20
  178.5 1.6 copy-start.16
  178.9 2.9 %copy-start.1 = (s32[512]{0:T(512)S(1)}, s32[512]{0:T(512)}, u32[]{:S(2)}) copy-start(s32[512]{0:T(512)} %param.31) | copy-start | bytes 6148
where the time goes:
time: 183 us; the launch traced here: 182 us
  local copies, waits for them, and re-layouts  55 us (30%)
  waiting for transfers between devices  41.5 us (23%)
  starting transfers between devices  34.5 us (19%)
  matrix products  26.9 us (15%)
  other arithmetic  22.6 us (12%)
    ppermute x4, waiting for transfers between devices, swapped(): lax.ppermute(x, axis, [(i, i ^ 1 << stride) for i in range(lax.axis_size(...  17.7 us
    another operation x4, local copies, waits for them, and re-layouts  13.2 us
    all_to_all x1, waiting for transfers between devices, body(): lax.all_to_all(cotangent, 'head', split_axis=1, concat_axis=0, tiled=True)  10.8 us
    ppermute x4, starting transfers between devices, swapped(): lax.ppermute(x, axis, [(i, i ^ 1 << stride) for i in range(lax.axis_size(...  10.6 us
    all_to_all x1, starting transfers between devices, body(): lax.all_to_all(key_rows, 'head', split_axis=1, concat_axis=0, tiled=True)  10.3 us
    all_to_all x1, waiting for transfers between devices, body(): lax.all_to_all(queries, 'head', split_axis=1, concat_axis=0, tiled=True)  9.99 us
    gather x5, local copies, waits for them, and re-layouts, settle(): pulled = jnp.take(arriving, slot_rank, axis=0)  7.41 us
    unnamed x58, local copies, waits for them, and re-layouts  5.03 us
  transfers between devices with their start and end apart: 8, of which 5 were waited for; matrix products, arithmetic and copies ran while one was open for 17% of the time, Pallas kernels for 0%

commit v1 on v0

v1 whole, which is shorter than its diff:
```python
import functools

import jax
import jax.numpy as jnp
import numpy as np
from jax import lax
from jax.experimental import pallas as pl
from jax.experimental.pallas import tpu as pltpu
from jax.sharding import PartitionSpec as P

HEAD_DIM = 128
BLOCK = 128
BIN = 4 * BLOCK
GROUP = 4
CHUNKS = 1 + GROUP
LANES = 2 * BLOCK
SCALE = HEAD_DIM ** -0.5
LOG2E = 1.4426950408889634
FAR = -1e30
MESH = pl.DeviceIdType.MESH
NT = (((1,), (1,)), ((), ()))


def dot(a, b, dims=(((1,), (0,)), ((), ()))):
    return lax.dot_general(a, b, dims, preferred_element_type=jnp.float32)


def fill_bias(bias, which, docs):
    row = lax.broadcasted_iota(jnp.int32, (BLOCK, BLOCK), 0)
    col = lax.broadcasted_iota(jnp.int32, (BLOCK, BLOCK), 1)
    causal = jnp.where(row <= col, 0.0, FAR)
    for half in range(2):
        for kb in range(2 * half + 2):
            for side in range(2):
                qb = 2 * half + side
                if kb == qb:
                    tile = causal
                elif kb > qb:
                    tile = jnp.full((BLOCK, BLOCK), FAR, jnp.float32)
                else:
                    tile = jnp.full((BLOCK, BLOCK), jnp.where(docs[kb] == docs[qb], 0.0, FAR), jnp.float32)
                bias[which, pl.ds(half * LANES + kb * BLOCK, BLOCK), pl.ds(side * BLOCK, BLOCK)] = tile


def head_grads(k, v, k_t, q, d, bias, which, grad_k, grad_v, first):
    parts = []
    for half in range(2):
        keys = (half + 1) * LANES
        rows = slice(half * LANES, (half + 1) * LANES)
        q_half, d_half = q[rows], d[rows]
        scores = dot(k[:keys], q_half, NT) * (SCALE * LOG2E) + bias[which, pl.ds(half * LANES, keys), :]
        scores = jnp.exp2(scores - jnp.max(scores, axis=0, keepdims=True))
        weights = scores * (1.0 / jnp.sum(scores, axis=0, keepdims=True))
        dweights = dot(v[:keys], d_half, NT)
        row_delta = jnp.sum(weights * dweights, axis=0, keepdims=True)
        dscores = (weights * (dweights - row_delta)).astype(jnp.bfloat16)
        add_v = dot(weights.astype(jnp.bfloat16), d_half)
        add_k = dot(dscores, q_half)
        if first and half == 0:
            grad_v[which, pl.ds(LANES, LANES), :] = jnp.zeros((LANES, HEAD_DIM), jnp.float32)
            grad_k[which, pl.ds(LANES, LANES), :] = jnp.zeros((LANES, HEAD_DIM), jnp.float32)
            grad_v[which, pl.ds(0, LANES), :] = add_v
            grad_k[which, pl.ds(0, LANES), :] = add_k
        else:
            grad_v[which, pl.ds(0, keys), :] += add_v
            grad_k[which, pl.ds(0, keys), :] += add_k
        parts.append(dot(k_t[:, :keys], dscores))
    return parts


def kernel(heads, bpd, *refs):
    sources, (route, doc), outs = refs[:4], refs[4:6], refs[6:9]
    xb, zs, zr = refs[9:14], refs[14:19], refs[19:24]
    k_t, bias, grad_k, grad_v, kept_q, route_s, doc_s = refs[24:31]
    x_send, x_recv, z_send, z_recv, own_sem, table_sem = refs[31:37]
    queries, key_rows, values, cotangent = sources
    me = lax.axis_index("head")
    dp = lax.axis_index("dp")
    mate = dp + 1 - 2 * (dp % 2)

    tables = [
        pltpu.make_async_copy(route, route_s, table_sem.at[0]),
        pltpu.make_async_copy(doc, doc_s, table_sem.at[1]),
    ]
    for copy in tables:
        copy.start()

    barrier = pltpu.get_barrier_semaphore()
    peers = [(me + step) % heads for step in range(1, heads)]
    for peer in peers:
        pl.semaphore_signal(barrier, inc=1, device_id=(dp, peer), device_id_type=MESH)
    pl.semaphore_signal(barrier, inc=1, device_id=(mate, me), device_id_type=MESH)

    def piece(chunk, which, peer):
        if chunk == 0:
            ref, first = (key_rows, values)[which], peer * HEAD_DIM
        else:
            ref, first = (queries, cotangent)[which], (peer * GROUP + chunk - 1) * HEAD_DIM
        return ref.at[:, pl.ds(pl.multiple_of(first, HEAD_DIM), HEAD_DIM)]

    def landing(chunk, which, block):
        return xb[chunk].at[which, block // 4, pl.ds(pl.multiple_of(block % 4 * BLOCK, BLOCK), BLOCK)]

    own = []
    for chunk in range(CHUNKS):
        for which in range(2):
            copy = pltpu.make_async_copy(
                piece(chunk, which, me), landing(chunk, which, me), own_sem.at[chunk, which]
            )
            copy.start()
            own.append(copy)
    pl.semaphore_wait(barrier, heads)

    sent = []
    for chunk in range(CHUNKS):
        for which in range(2):
            for step, peer in enumerate(peers):
                copy = pltpu.make_async_remote_copy(
                    src_ref=piece(chunk, which, peer),
                    dst_ref=landing(chunk, which, me),
                    send_sem=x_send.at[chunk, which, step],
                    recv_sem=x_recv.at[chunk, which, step],
                    device_id=(dp, peer),
                    device_id_type=MESH,
                )
                copy.start()
                sent.append(copy)

    for copy in tables:
        copy.wait()
    moved = jnp.where(route_s[0, dp * bpd] != dp, 0, 1)
    mate_moved = jnp.where(route_s[0, mate * bpd] != mate, 0, 1)
    kept = 1 - moved
    kept_docs = [doc_s[dp * bpd + kept * 4 + i] for i in range(4)]
    come_docs = [doc_s[mate * bpd + mate_moved * 4 + i] for i in range(4)]
    fill_bias(bias, 0, kept_docs)
    fill_bias(bias, 1, come_docs)

    def settle(stays, comes):
        return [jnp.where(moved == slot, comes, stays) for slot in range(2)]

    def keep(chunk):
        parts = head_grads(
            xb[0][0, kept], xb[0][1, kept], k_t[0], xb[chunk][0, kept], xb[chunk][1, kept],
            bias, 0, grad_k, grad_v, chunk == 1,
        )
        for half, part in enumerate(parts):
            kept_q[chunk - 1, pl.ds(half * LANES, LANES), :] = (part * SCALE).T

    def come(chunk):
        parts = head_grads(
            zr[0][0], zr[0][1], k_t[1], zr[chunk][0], zr[chunk][1],
            bias, 1, grad_k, grad_v, chunk == 1,
        )
        for half, part in enumerate(parts):
            stays = kept_q[chunk - 1, pl.ds(half * LANES, LANES), :]
            for slot, rows in enumerate(settle(stays, (part * SCALE).T)):
                outs[0][pl.ds(slot * BIN + half * LANES, LANES), pl.ds((chunk - 1) * HEAD_DIM, HEAD_DIM)] = (
                    rows.astype(jnp.bfloat16)
                )

    passed = []
    for chunk in range(CHUNKS):
        for copy in own[2 * chunk : 2 * chunk + 2]:
            copy.wait()
        for copy in sent[2 * (heads - 1) * chunk : 2 * (heads - 1) * (chunk + 1)]:
            copy.wait_recv()
        zs[chunk][...] = xb[chunk][:, moved]
        copy = pltpu.make_async_remote_copy(
            src_ref=zs[chunk],
            dst_ref=zr[chunk],
            send_sem=z_send.at[chunk],
            recv_sem=z_recv.at[chunk],
            device_id=(mate, me),
            device_id_type=MESH,
        )
        copy.start()
        passed.append(copy)
        if chunk == 0:
            k_t[0] = xb[0][0, kept].T
        else:
            keep(chunk)
            passed[chunk - 1].wait_recv()
            if chunk == 1:
                k_t[1] = zr[0][0].T
            else:
                come(chunk - 1)
    passed[-1].wait_recv()
    come(CHUNKS - 1)
    for out, total, scale in ((outs[1], grad_k, SCALE), (outs[2], grad_v, 1.0)):
        for slot, rows in enumerate(settle(total[0] * scale, total[1] * scale)):
            out[pl.ds(slot * BIN, BIN), :] = rows.astype(jnp.bfloat16)
    for copy in sent + passed:
        copy.wait_send()


def body(queries, key_rows, values, cotangent, block_route, doc_start):
    heads = lax.axis_size("head")
    bpd = block_route.shape[0] // lax.axis_size("dp")
    rows = bpd * BLOCK
    anywhere = pl.BlockSpec(memory_space=pl.ANY)
    vmem = pl.BlockSpec(memory_space=pltpu.VMEM)
    half, whole = (2, BIN, HEAD_DIM), (2, 2, BIN, HEAD_DIM)
    return pl.pallas_call(
        functools.partial(kernel, heads, bpd),
        out_shape=(
            jax.ShapeDtypeStruct((rows, GROUP * HEAD_DIM), jnp.bfloat16),
            jax.ShapeDtypeStruct((rows, HEAD_DIM), jnp.bfloat16),
            jax.ShapeDtypeStruct((rows, HEAD_DIM), jnp.bfloat16),
        ),
        in_specs=[anywhere] * 6,
        out_specs=[vmem] * 3,
        scratch_shapes=[pltpu.VMEM(whole, jnp.bfloat16)] * CHUNKS
        + [pltpu.VMEM(half, jnp.bfloat16)] * (2 * CHUNKS)
        + [
            pltpu.VMEM((2, HEAD_DIM, BIN), jnp.bfloat16),
            pltpu.VMEM((2, 3 * LANES, LANES), jnp.float32),
            pltpu.VMEM(half, jnp.float32),
            pltpu.VMEM(half, jnp.float32),
            pltpu.VMEM((GROUP, BIN, HEAD_DIM), jnp.float32),
            pltpu.SMEM((2, block_route.shape[0]), jnp.int32),
            pltpu.SMEM(doc_start.shape, jnp.int32),
            pltpu.SemaphoreType.DMA((CHUNKS, 2, heads - 1)),
            pltpu.SemaphoreType.DMA((CHUNKS, 2, heads - 1)),
            pltpu.SemaphoreType.DMA((CHUNKS,)),
            pltpu.SemaphoreType.DMA((CHUNKS,)),
            pltpu.SemaphoreType.DMA((CHUNKS, 2)),
            pltpu.SemaphoreType.DMA((2,)),
        ],
        compiler_params=pltpu.CompilerParams(
            collective_id=0, has_side_effects=True, vmem_limit_bytes=60 * 2**20
        ),
    )(queries, key_rows, values, cotangent, block_route.T, doc_start)


def solution(mesh):
    tokens = P(("dp", "head"), None)
    return jax.shard_map(
        body,
        mesh=mesh,
        in_specs=(tokens, tokens, tokens, tokens, P(), P()),
        out_specs=(P("dp", "head"), P("dp", "head"), P("dp", "head")),
        check_vma=False,
    )
```

time: 183 us -> 54.6 us (0.30)
  local copies, waits for them, and re-layouts: 55 us -> 4.05 us
  Pallas kernels: 0 us -> 48.9 us
  waiting for transfers between devices: 41.5 us -> 0 us
  starting transfers between devices: 34.5 us -> 0 us
  matrix products: 26.9 us -> 0 us
  other arithmetic: 22.6 us -> 0 us
    pallas_call x0 -> x1, Pallas kernels: none -> 48.9 us  [body(): pl.pallas_call(functools.partial(kernel, heads, bpd), out_shape=(jax.Shap...]
    dot_general x11 -> x0, matrix products: 26.9 us -> none  [the longest x1 4.89 us: attend(): jnp.einsum('ts,tqcgd->sqcgd', query_mix, attended_tiles, precision=highest)]
    all_to_all x4 -> x0, starting transfers between devices: 24 us -> none  [the longest x1 10.3 us: body(): lax.all_to_all(key_rows, 'head', split_axis=1, concat_axis=0, tiled=True)]
    all_to_all x4 -> x0, waiting for transfers between devices: 23.8 us -> none  [the longest x1 10.8 us: body(): lax.all_to_all(cotangent, 'head', split_axis=1, concat_axis=0, tiled=True)]
    gather x22 -> x0, local copies, waits for them, and re-layouts: 22.1 us -> none  [the longest x5 7.41 us: settle(): pulled = jnp.take(arriving, slot_rank, axis=0)]
    ppermute x4 -> x0, waiting for transfers between devices: 17.7 us -> none  [swapped(): lax.ppermute(x, axis, [(i, i ^ 1 << stride) for i in range(lax.axis_size(...]
    another operation x5 -> x0, local copies, waits for them, and re-layouts: 13.2 us -> none
    ppermute x4 -> x0, starting transfers between devices: 10.6 us -> none  [swapped(): lax.ppermute(x, axis, [(i, i ^ 1 << stride) for i in range(lax.axis_size(...]
  transfers between devices with their start and end apart: 8 -> 0, of which waited for: 5 -> 0; matrix products, arithmetic and copies ran while one was open for 17% -> 0% of each run, Pallas kernels for 0% -> 0%
where the time goes in v1:
time: 54.6 us; the launch traced here: 53.6 us
  Pallas kernels  48.9 us (90%)
  local copies, waits for them, and re-layouts  4.05 us (7%)
  between operations  0.65 us (1%)
    pallas_call x1, Pallas kernels, body(): pl.pallas_call(functools.partial(kernel, heads, bpd), out_shape=(jax.Shap...  48.9 us
    unnamed x7, local copies, waits for them, and re-layouts  4.05 us

profile of v1, /device:TPU:1, one launch (start us, length us, event | category | flops | bytes accessed | tf_op | source)
XLA Modules:
  0.0 53.6 jit_solution(1284739547305303999)
XLA Ops:
  0.6 48.9 %shard_map.85 = (bf16[1024,512]{1,0:T(8,128)(2,1)}, bf16[1024,128]{1,0:T(8,128)(2,1)}, bf16[1024,128]{1,0:T(8,128)(2,1)}) custom-call(bf16[128,4096]{1,0:T(8,128)(2,1)} %refs_0_.1, bf16[128,1024]{1,0:T(8,128)(2,1)} %refs_1_.1, bf16[128,1024]{1,0:T(8,128)(2,1)} %refs_2_.1, bf16[128,4096]{1,0:T(8,128)(2,1)} %refs_3_.1, s32[2,512]{1,0:T(2,128)} %bitcast.1, ...), custom_call_target="tpu_custom_call" | custom-call | tf_op jit(solution)/shard_map/pallas_call | solution.py:204
  49.5 0.0 copy-start.1
  49.5 2.3 %copy.12 = bf16[1024,512]{1,0:T(8,128)(2,1)} copy(bf16[1024,512]{1,0:T(8,128)(2,1)} %get-tuple-element.6) | data formatting | bytes 2097152
  51.8 0.0 copy-done.1
  51.8 0.0 copy-start
  51.8 0.7 %copy.13 = bf16[1024,128]{1,0:T(8,128)(2,1)} copy(bf16[1024,128]{1,0:T(8,128)(2,1)S(1)} %copy-done.1) | data formatting | bytes 524288
  52.5 0.3 copy-done
  52.9 0.7 %copy.14 = bf16[1024,128]{1,0:T(8,128)(2,1)} copy(bf16[1024,128]{1,0:T(8,128)(2,1)S(1)} %copy-done) | data formatting | bytes 524288
Async XLA Ops:
  49.5 2.3 %copy-start.1 = (bf16[1024,128]{1,0:T(8,128)(2,1)S(1)}, bf16[1024,128]{1,0:T(8,128)(2,1)}, u32[]{:S(2)}) copy-start(bf16[1024,128]{1,0:T(8,128)(2,1)} %get-tuple-element.7) | copy-start | bytes 786436
  51.8 1.0 %copy-start = (bf16[1024,128]{1,0:T(8,128)(2,1)S(1)}, bf16[1024,128]{1,0:T(8,128)(2,1)}, u32[]{:S(2)}) copy-start(bf16[1024,128]{1,0:T(8,128)(2,1)} %get-tuple-element.8) | copy-start | bytes 786436

commit v2 on v1

v2 whole, which is shorter than its diff:
```python
import functools

import jax
import jax.numpy as jnp
import numpy as np
from jax import lax
from jax.experimental import pallas as pl
from jax.experimental.pallas import tpu as pltpu
from jax.sharding import PartitionSpec as P

HEAD_DIM = 128
BLOCK = 128
BIN = 4 * BLOCK
GROUP = 4
CHUNKS = 1 + GROUP
LANES = 2 * BLOCK
ARRAYS = 2 * CHUNKS
SCALE = HEAD_DIM ** -0.5
LOG2E = 1.4426950408889634
FAR = -1e30
MESH = pl.DeviceIdType.MESH
NT = (((1,), (1,)), ((), ()))


def dot(a, b, dims=(((1,), (0,)), ((), ()))):
    return lax.dot_general(a, b, dims, preferred_element_type=jnp.float32)


def fill_bias(bias, which, docs):
    row = lax.broadcasted_iota(jnp.int32, (BLOCK, BLOCK), 0)
    col = lax.broadcasted_iota(jnp.int32, (BLOCK, BLOCK), 1)
    causal = jnp.where(row <= col, 0.0, FAR)
    for half in range(2):
        for kb in range(2 * half + 2):
            for side in range(2):
                qb = 2 * half + side
                if kb == qb:
                    tile = causal
                elif kb > qb:
                    tile = jnp.full((BLOCK, BLOCK), FAR, jnp.float32)
                else:
                    tile = jnp.full((BLOCK, BLOCK), jnp.where(docs[kb] == docs[qb], 0.0, FAR), jnp.float32)
                bias[which, pl.ds(half * LANES + kb * BLOCK, BLOCK), pl.ds(side * BLOCK, BLOCK)] = tile


def halves():
    for half in range(2):
        yield pl.ds(half * LANES, LANES), half * LANES, (half + 1) * LANES


def weigh(k, q, bias, weights):
    for _, first, keys in halves():
        scores = dot(k[:keys], q[first : first + LANES], NT) * (SCALE * LOG2E) + bias[pl.ds(first, keys), :]
        scores = jnp.exp2(scores - jnp.max(scores, axis=0, keepdims=True))
        weights[pl.ds(first, keys), :] = scores * (1.0 / jnp.sum(scores, axis=0, keepdims=True))


def spread(v, k_t, q, d, weights, grad_k, grad_v, opens):
    parts = []
    for rows, first, keys in halves():
        q_half, d_half = q[first : first + LANES], d[first : first + LANES]
        share = weights[pl.ds(first, keys), :]
        dweights = dot(v[:keys], d_half, NT)
        row_delta = jnp.sum(share * dweights, axis=0, keepdims=True)
        dscores = (share * (dweights - row_delta)).astype(jnp.bfloat16)
        add_v = dot(share.astype(jnp.bfloat16), d_half)
        add_k = dot(dscores, q_half)
        if opens and first == 0:
            later = pl.ds(LANES, LANES)
            for total, add in ((grad_v, add_v), (grad_k, add_k)):
                total[later, :] = jnp.zeros((LANES, HEAD_DIM), jnp.float32)
                total[pl.ds(0, LANES), :] = add
        else:
            grad_v[pl.ds(0, keys), :] += add_v
            grad_k[pl.ds(0, keys), :] += add_k
        parts.append((rows, first, (dot(k_t[:, :keys], dscores) * SCALE).T))
    return parts


def kernel(heads, bpd, *refs):
    (queries, key_rows, values, cotangent), (route, doc), (out_q, out_k, out_v) = refs[:4], refs[4:6], refs[6:9]
    xb, zs, zr = (refs[9 + n * ARRAYS : 9 + (n + 1) * ARRAYS] for n in range(3))
    k_t, bias, weights, grad_k, grad_v, kept_q, route_s, doc_s = refs[39:47]
    x_send, x_recv, z_send, z_recv, own_sem, table_sem = refs[47:53]
    me = lax.axis_index("head")
    dp = lax.axis_index("dp")
    mate = dp + 1 - 2 * (dp % 2)
    peers = [(me + step) % heads for step in range(1, heads)]

    barrier = pltpu.get_barrier_semaphore()
    for peer in peers:
        pl.semaphore_signal(barrier, inc=1, device_id=(dp, peer), device_id_type=MESH)
    pl.semaphore_signal(barrier, inc=1, device_id=(mate, me), device_id_type=MESH)

    tables = [
        pltpu.make_async_copy(route, route_s, table_sem.at[0]),
        pltpu.make_async_copy(doc, doc_s, table_sem.at[1]),
    ]
    for copy in tables:
        copy.start()

    def source(n, peer):
        if n < 2:
            ref, first = (key_rows, values)[n], peer * HEAD_DIM
        else:
            ref, first = (queries, cotangent)[n % 2], (peer * GROUP + n // 2 - 1) * HEAD_DIM
        return ref.at[:, pl.ds(pl.multiple_of(first, HEAD_DIM), HEAD_DIM)]

    def landing(n):
        return xb[n].at[me // 4, pl.ds(pl.multiple_of(me % 4 * BLOCK, BLOCK), BLOCK)]

    own, sent = [], []
    for n in range(ARRAYS):
        copy = pltpu.make_async_copy(source(n, me), landing(n), own_sem.at[n])
        copy.start()
        own.append(copy)
    pl.semaphore_wait(barrier, heads)
    for n in range(ARRAYS):
        sent.append([])
        for step, peer in enumerate(peers):
            copy = pltpu.make_async_remote_copy(
                src_ref=source(n, peer),
                dst_ref=landing(n),
                send_sem=x_send.at[n, step],
                recv_sem=x_recv.at[n, step],
                device_id=(dp, peer),
                device_id_type=MESH,
            )
            copy.start()
            sent[-1].append(copy)

    for copy in tables:
        copy.wait()
    moved = jnp.where(route_s[0, dp * bpd] != dp, 0, 1)
    mate_moved = jnp.where(route_s[0, mate * bpd] != mate, 0, 1)
    kept = 1 - moved
    fill_bias(bias, 0, [doc_s[dp * bpd + kept * 4 + i] for i in range(4)])
    fill_bias(bias, 1, [doc_s[mate * bpd + mate_moved * 4 + i] for i in range(4)])

    def settle(stays, comes):
        return [jnp.where(moved == slot, comes, stays) for slot in range(2)]

    def work(side, n):
        def bin_of(n):
            return zr[n][...] if side else xb[n][kept]

        if n == 0:
            k_t[side] = bin_of(0).T
        elif n > 1 and n % 2 == 0:
            weigh(bin_of(0), bin_of(n), bias.at[side], weights.at[side])
        elif n > 1:
            parts = spread(
                bin_of(1), k_t[side], bin_of(n - 1), bin_of(n), weights.at[side],
                grad_k.at[side], grad_v.at[side], n == 3,
            )
            head = n // 2 - 1
            for rows, first, part in parts:
                if side == 0:
                    kept_q[head, rows, :] = part
                    continue
                for slot, settled in enumerate(settle(kept_q[head, rows, :], part)):
                    out_q[pl.ds(slot * BIN + first, LANES), pl.ds(head * HEAD_DIM, HEAD_DIM)] = settled.astype(
                        jnp.bfloat16
                    )

    passed = []
    for n in range(ARRAYS):
        own[n].wait()
        for copy in sent[n]:
            copy.wait_recv()
        zs[n][...] = xb[n][moved]
        copy = pltpu.make_async_remote_copy(
            src_ref=zs[n],
            dst_ref=zr[n],
            send_sem=z_send.at[n],
            recv_sem=z_recv.at[n],
            device_id=(mate, me),
            device_id_type=MESH,
        )
        copy.start()
        passed.append(copy)
        work(0, n)
        if n > 0:
            passed[n - 1].wait_recv()
            work(1, n - 1)
    passed[-1].wait_recv()
    work(1, ARRAYS - 1)
    for out, total, scale in ((out_k, grad_k, SCALE), (out_v, grad_v, 1.0)):
        for slot, settled in enumerate(settle(total[0] * scale, total[1] * scale)):
            out[pl.ds(slot * BIN, BIN), :] = settled.astype(jnp.bfloat16)
    for copy in [copy for group in sent for copy in group] + passed:
        copy.wait_send()


def write(*refs):
    copies = [pltpu.make_async_copy(refs[n], refs[n + 3], refs[6].at[n]) for n in range(3)]
    for copy in copies:
        copy.start()
    for copy in copies:
        copy.wait()


def body(queries, key_rows, values, cotangent, block_route, doc_start):
    heads = lax.axis_size("head")
    bpd = block_route.shape[0] // lax.axis_size("dp")
    rows = bpd * BLOCK
    anywhere = pl.BlockSpec(memory_space=pl.ANY)
    vmem = pl.BlockSpec(memory_space=pltpu.VMEM)
    shapes = [(rows, GROUP * HEAD_DIM), (rows, HEAD_DIM), (rows, HEAD_DIM)]
    arguments = [
        pltpu.with_memory_space_constraint(x, pltpu.HBM)
        for x in (queries, key_rows, values, cotangent, block_route.T, doc_start)
    ]
    held = pl.pallas_call(
        functools.partial(kernel, heads, bpd),
        out_shape=[pltpu.VMEM(shape, jnp.bfloat16) for shape in shapes],
        in_specs=[anywhere] * 6,
        out_specs=[vmem] * 3,
        scratch_shapes=[pltpu.VMEM((2, BIN, HEAD_DIM), jnp.bfloat16)] * ARRAYS
        + [pltpu.VMEM((BIN, HEAD_DIM), jnp.bfloat16)] * (2 * ARRAYS)
        + [
            pltpu.VMEM((2, HEAD_DIM, BIN), jnp.bfloat16),
            pltpu.VMEM((2, 3 * LANES, LANES), jnp.float32),
            pltpu.VMEM((2, 3 * LANES, LANES), jnp.float32),
            pltpu.VMEM((2, BIN, HEAD_DIM), jnp.float32),
            pltpu.VMEM((2, BIN, HEAD_DIM), jnp.float32),
            pltpu.VMEM((GROUP, BIN, HEAD_DIM), jnp.float32),
            pltpu.SMEM((2, block_route.shape[0]), jnp.int32),
            pltpu.SMEM(doc_start.shape, jnp.int32),
            pltpu.SemaphoreType.DMA((ARRAYS, heads - 1)),
            pltpu.SemaphoreType.DMA((ARRAYS, heads - 1)),
            pltpu.SemaphoreType.DMA((ARRAYS,)),
            pltpu.SemaphoreType.DMA((ARRAYS,)),
            pltpu.SemaphoreType.DMA((ARRAYS,)),
            pltpu.SemaphoreType.DMA((2,)),
        ],
        compiler_params=pltpu.CompilerParams(
            collective_id=0, has_side_effects=True, vmem_limit_bytes=40 * 2**20
        ),
    )(*arguments)
    return pl.pallas_call(
        write,
        out_shape=[jax.ShapeDtypeStruct(shape, jnp.bfloat16) for shape in shapes],
        in_specs=[vmem] * 3,
        out_specs=[anywhere] * 3,
        scratch_shapes=[pltpu.SemaphoreType.DMA((3,))],
        compiler_params=pltpu.CompilerParams(vmem_limit_bytes=2**20),
    )(*(pltpu.with_memory_space_constraint(x, pltpu.VMEM) for x in held))


def solution(mesh):
    tokens = P(("dp", "head"), None)
    return jax.shard_map(
        body,
        mesh=mesh,
        in_specs=(tokens, tokens, tokens, tokens, P(), P()),
        out_specs=(P("dp", "head"), P("dp", "head"), P("dp", "head")),
        check_vma=False,
    )
```

time: 54.6 us -> 48.8 us (0.89); the launches traced: 53.6 us -> 48.6 us
  local copies, waits for them, and re-layouts: 4.05 us -> 0 us
  Pallas kernels: 48.9 us -> 48 us
    unnamed x7 -> x0, local copies, waits for them, and re-layouts: 4.05 us -> none
    pallas_call x1 -> x2, Pallas kernels: 48.9 us -> 48 us  [the longest x1 46.8 us: body(): pl.pallas_call(functools.partial(kernel, heads, bpd), out_shape=[pltpu.VM...]
where the time goes in v2:
time: 48.8 us; the launch traced here: 48.6 us
  Pallas kernels  48 us (98%)
  between operations  0.64 us (1%)
    pallas_call x1, Pallas kernels, body(): pl.pallas_call(functools.partial(kernel, heads, bpd), out_shape=[pltpu.VM...  46.8 us
    pallas_call x1, Pallas kernels, body(): pl.pallas_call(write, out_shape=[jax.ShapeDtypeStruct(shape, jnp.bfloat16...  1.16 us

profile of v2, /device:TPU:1, one launch (start us, length us, event | category | flops | bytes accessed | tf_op | source)
XLA Modules:
  0.0 48.6 jit_solution(8646764523727573230)
XLA Ops:
  0.6 46.8 %shard_map.85 = (bf16[1024,512]{1,0:T(8,128)(2,1)S(1)}, bf16[1024,128]{1,0:T(8,128)(2,1)S(1)}, bf16[1024,128]{1,0:T(8,128)(2,1)S(1)}) custom-call(bf16[128,4096]{1,0:T(8,128)(2,1)} %refs_0_.1, bf16[128,1024]{1,0:T(8,128)(2,1)} %refs_1_.1, bf16[128,1024]{1,0:T(8,128)(2,1)} %refs_2_.1, bf16[128,4096]{1,0:T(8,128)(2,1)} %refs_3_.1, s32[2,512]{1,0:T(2,128)} %bitcast.1, ...), custom_call_target="tpu_custom_call" | custom-call | tf_op jit(solution)/shard_map/pallas_call | solution.py:214
  47.5 1.2 %shard_map.86 = (bf16[1024,512]{1,0:T(8,128)(2,1)}, bf16[1024,128]{1,0:T(8,128)(2,1)}, bf16[1024,128]{1,0:T(8,128)(2,1)}) custom-call(bf16[1024,512]{1,0:T(8,128)(2,1)S(1)} %get-tuple-element.6.refs_0_, bf16[1024,128]{1,0:T(8,128)(2,1)S(1)} %get-tuple-element.7.refs_1_, bf16[1024,128]{1,0:T(8,128)(2,1)S(1)} %get-tuple-element.8.refs_2_), custom_call_target="tpu_custom_call" | custom-call | tf_op jit(solution)/shard_map/pallas_call | solution.py:241

commit v3 on v2

--- a/solution.py
+++ b/solution.py
@@ -43,38 +43,26 @@
                 bias[which, pl.ds(half * LANES + kb * BLOCK, BLOCK), pl.ds(side * BLOCK, BLOCK)] = tile
 
 
-def halves():
+def weigh(k, q, bias, weights):
     for half in range(2):
-        yield pl.ds(half * LANES, LANES), half * LANES, (half + 1) * LANES
-
-
-def weigh(k, q, bias, weights):
-    for _, first, keys in halves():
+        first, keys = half * LANES, (half + 1) * LANES
         scores = dot(k[:keys], q[first : first + LANES], NT) * (SCALE * LOG2E) + bias[pl.ds(first, keys), :]
         scores = jnp.exp2(scores - jnp.max(scores, axis=0, keepdims=True))
         weights[pl.ds(first, keys), :] = scores * (1.0 / jnp.sum(scores, axis=0, keepdims=True))
 
 
-def spread(v, k_t, q, d, weights, grad_k, grad_v, opens):
-    parts = []
-    for rows, first, keys in halves():
-        q_half, d_half = q[first : first + LANES], d[first : first + LANES]
-        share = weights[pl.ds(first, keys), :]
-        dweights = dot(v[:keys], d_half, NT)
-        row_delta = jnp.sum(share * dweights, axis=0, keepdims=True)
-        dscores = (share * (dweights - row_delta)).astype(jnp.bfloat16)
-        add_v = dot(share.astype(jnp.bfloat16), d_half)
-        add_k = dot(dscores, q_half)
-        if opens and first == 0:
-            later = pl.ds(LANES, LANES)
-            for total, add in ((grad_v, add_v), (grad_k, add_k)):
-                total[later, :] = jnp.zeros((LANES, HEAD_DIM), jnp.float32)
-                total[pl.ds(0, LANES), :] = add
+def spread(half, v, k_t, q, d, weights, grad_k, grad_v, opens):
+    keys = (half + 1) * LANES
+    share = weights[pl.ds(half * LANES, keys), :]
+    dweights = dot(v[:keys], d, NT)
+    row_delta = jnp.sum(share * dweights, axis=0, keepdims=True)
+    dscores = (share * (dweights - row_delta)).astype(jnp.bfloat16)
+    for total, add in ((grad_v, dot(share.astype(jnp.bfloat16), d)), (grad_k, dot(dscores, q))):
+        if opens and half == 1:
+            total[...] = add
         else:
-            grad_v[pl.ds(0, keys), :] += add_v
-            grad_k[pl.ds(0, keys), :] += add_k
-        parts.append((rows, first, (dot(k_t[:, :keys], dscores) * SCALE).T))
-    return parts
+            total[pl.ds(0, keys), :] += add
+    return (dot(k_t[:, :keys], dscores) * SCALE).T
 
 
 def kernel(heads, bpd, *refs):
@@ -140,55 +128,67 @@
     def settle(stays, comes):
         return [jnp.where(moved == slot, comes, stays) for slot in range(2)]
 
-    def work(side, n):
+    def work(side, n, half):
+        rows = pl.ds(half * LANES, LANES)
+
         def bin_of(n):
             return zr[n][...] if side else xb[n][kept]
 
-        if n == 0:
+        def half_of(n):
+            return zr[n][rows, :] if side else xb[n][kept, rows, :]
+
+        if n == 0 and half == 0:
             k_t[side] = bin_of(0).T
-        elif n > 1 and n % 2 == 0:
+        elif n > 1 and n % 2 == 0 and half == 0:
             weigh(bin_of(0), bin_of(n), bias.at[side], weights.at[side])
-        elif n > 1:
-            parts = spread(
-                bin_of(1), k_t[side], bin_of(n - 1), bin_of(n), weights.at[side],
+        elif n > 1 and n % 2:
+            part = spread(
+                half, bin_of(1), k_t[side], half_of(n - 1), half_of(n), weights.at[side],
                 grad_k.at[side], grad_v.at[side], n == 3,
             )
             head = n // 2 - 1
-            for rows, first, part in parts:
-                if side == 0:
-                    kept_q[head, rows, :] = part
-                    continue
-                for slot, settled in enumerate(settle(kept_q[head, rows, :], part)):
-                    out_q[pl.ds(slot * BIN + first, LANES), pl.ds(head * HEAD_DIM, HEAD_DIM)] = settled.astype(
-                        jnp.bfloat16
-                    )
-
-    passed = []
+            if side == 0:
+                kept_q[head, rows, :] = part
+                return
+            for slot, settled in enumerate(settle(kept_q[head, rows, :], part)):
+                out_q[pl.ds(slot * BIN + half * LANES, LANES), pl.ds(head * HEAD_DIM, HEAD_DIM)] = settled.astype(
+                    jnp.bfloat16
+                )
+
+    def forward(n, half):
+        rows = pl.ds(0, BIN) if half is None else pl.ds(half * LANES, LANES)
+        copy = pltpu.make_async_remote_copy(
+            src_ref=zs[n].at[rows],
+            dst_ref=zr[n].at[rows],
+            send_sem=z_send.at[n, half or 0],
+            recv_sem=z_recv.at[n, half or 0],
+            device_id=(mate, me),
+            device_id_type=MESH,
+        )
+        copy.start()
+        return copy
+
+    last, passed = ARRAYS - 1, []
     for n in range(ARRAYS):
         own[n].wait()
         for copy in sent[n]:
             copy.wait_recv()
         zs[n][...] = xb[n][moved]
-        copy = pltpu.make_async_remote_copy(
-            src_ref=zs[n],
-            dst_ref=zr[n],
-            send_sem=z_send.at[n],
-            recv_sem=z_recv.at[n],
-            device_id=(mate, me),
-            device_id_type=MESH,
-        )
-        copy.start()
-        passed.append(copy)
-        work(0, n)
+        passed.append([forward(n, half) for half in ((1, 0) if n == last else (None,))])
+        for half in (1, 0):
+            work(0, n, half)
         if n > 0:
-            passed[n - 1].wait_recv()
-            work(1, n - 1)
-    passed[-1].wait_recv()
-    work(1, ARRAYS - 1)
-    for out, total, scale in ((out_k, grad_k, SCALE), (out_v, grad_v, 1.0)):
-        for slot, settled in enumerate(settle(total[0] * scale, total[1] * scale)):
-            out[pl.ds(slot * BIN, BIN), :] = settled.astype(jnp.bfloat16)
-    for copy in [copy for group in sent for copy in group] + passed:
+            passed[n - 1][0].wait_recv()
+            for half in (1, 0):
+                work(1, n - 1, half)
+    for half, copy in zip((1, 0), passed[last]):
+        copy.wait_recv()
+        work(1, last, half)
+        rows = pl.ds(half * LANES, LANES)
+        for out, total, scale in ((out_k, grad_k, SCALE), (out_v, grad_v, 1.0)):
+            for slot, settled in enumerate(settle(total[0, rows, :] * scale, total[1, rows, :] * scale)):
+                out[pl.ds(slot * BIN + half * LANES, LANES), :] = settled.astype(jnp.bfloat16)
+    for copy in [copy for group in sent + passed for copy in group]:
         copy.wait_send()
 
 
@@ -229,8 +229,8 @@
             pltpu.SMEM(doc_start.shape, jnp.int32),
             pltpu.SemaphoreType.DMA((ARRAYS, heads - 1)),
             pltpu.SemaphoreType.DMA((ARRAYS, heads - 1)),
-            pltpu.SemaphoreType.DMA((ARRAYS,)),
-            pltpu.SemaphoreType.DMA((ARRAYS,)),
+            pltpu.SemaphoreType.DMA((ARRAYS, 2)),
+            pltpu.SemaphoreType.DMA((ARRAYS, 2)),
             pltpu.SemaphoreType.DMA((ARRAYS,)),
             pltpu.SemaphoreType.DMA((2,)),
         ],

time: 48.8 us -> 48.6 us (level)
  no operation moved by 1% of the time
where the time goes in v3:
time: 48.6 us; the launch traced here: 48.4 us
  Pallas kernels  47.7 us (98%)
  between operations  0.64 us (1%)
    pallas_call x1, Pallas kernels, body(): pl.pallas_call(functools.partial(kernel, heads, bpd), out_shape=[pltpu.VM...  46.6 us
    pallas_call x1, Pallas kernels, body(): pl.pallas_call(write, out_shape=[jax.ShapeDtypeStruct(shape, jnp.bfloat16...  1.16 us

profile of v3, /device:TPU:1, one launch (start us, length us, event | category | flops | bytes accessed | tf_op | source)
XLA Modules:
  0.0 48.4 jit_solution(332416995058483736)
XLA Ops:
  0.6 46.6 %shard_map.85 = (bf16[1024,512]{1,0:T(8,128)(2,1)S(1)}, bf16[1024,128]{1,0:T(8,128)(2,1)S(1)}, bf16[1024,128]{1,0:T(8,128)(2,1)S(1)}) custom-call(bf16[128,4096]{1,0:T(8,128)(2,1)} %refs_0_.1, bf16[128,1024]{1,0:T(8,128)(2,1)} %refs_1_.1, bf16[128,1024]{1,0:T(8,128)(2,1)} %refs_2_.1, bf16[128,4096]{1,0:T(8,128)(2,1)} %refs_3_.1, s32[2,512]{1,0:T(2,128)} %bitcast.1, ...), custom_call_target="tpu_custom_call" | custom-call | tf_op jit(solution)/shard_map/pallas_call | solution.py:214
  47.2 1.2 %shard_map.86 = (bf16[1024,512]{1,0:T(8,128)(2,1)}, bf16[1024,128]{1,0:T(8,128)(2,1)}, bf16[1024,128]{1,0:T(8,128)(2,1)}) custom-call(bf16[1024,512]{1,0:T(8,128)(2,1)S(1)} %get-tuple-element.6.refs_0_, bf16[1024,128]{1,0:T(8,128)(2,1)S(1)} %get-tuple-element.7.refs_1_, bf16[1024,128]{1,0:T(8,128)(2,1)S(1)} %get-tuple-element.8.refs_2_), custom_call_target="tpu_custom_call" | custom-call | tf_op jit(solution)/shard_map/pallas_call | solution.py:241

commit v4 on v3

--- a/solution.py
+++ b/solution.py
@@ -84,9 +84,6 @@
         pltpu.make_async_copy(route, route_s, table_sem.at[0]),
         pltpu.make_async_copy(doc, doc_s, table_sem.at[1]),
     ]
-    for copy in tables:
-        copy.start()
-
     def source(n, peer):
         if n < 2:
             ref, first = (key_rows, values)[n], peer * HEAD_DIM
@@ -98,10 +95,6 @@
         return xb[n].at[me // 4, pl.ds(pl.multiple_of(me % 4 * BLOCK, BLOCK), BLOCK)]
 
     own, sent = [], []
-    for n in range(ARRAYS):
-        copy = pltpu.make_async_copy(source(n, me), landing(n), own_sem.at[n])
-        copy.start()
-        own.append(copy)
     pl.semaphore_wait(barrier, heads)
     for n in range(ARRAYS):
         sent.append([])
@@ -116,6 +109,12 @@
             )
             copy.start()
             sent[-1].append(copy)
+        copy = pltpu.make_async_copy(source(n, me), landing(n), own_sem.at[n])
+        copy.start()
+        own.append(copy)
+        if n == 0:
+            for copy in tables:
+                copy.start()
 
     for copy in tables:
         copy.wait()

time: 48.6 us -> 48.6 us (level)
  no operation moved by 1% of the time
where the time goes in v4:
time: 48.6 us; the launch traced here: 48.4 us
  Pallas kernels  47.7 us (98%)
  between operations  0.64 us (1%)
    pallas_call x1, Pallas kernels, body(): pl.pallas_call(functools.partial(kernel, heads, bpd), out_shape=[pltpu.VM...  46.6 us
    pallas_call x1, Pallas kernels, body(): pl.pallas_call(write, out_shape=[jax.ShapeDtypeStruct(shape, jnp.bfloat16...  1.16 us

profile of v4, /device:TPU:1, one launch (start us, length us, event | category | flops | bytes accessed | tf_op | source)
XLA Modules:
  0.0 48.4 jit_solution(11254621433176640418)
XLA Ops:
  0.6 46.6 %shard_map.85 = (bf16[1024,512]{1,0:T(8,128)(2,1)S(1)}, bf16[1024,128]{1,0:T(8,128)(2,1)S(1)}, bf16[1024,128]{1,0:T(8,128)(2,1)S(1)}) custom-call(bf16[128,4096]{1,0:T(8,128)(2,1)} %refs_0_.1, bf16[128,1024]{1,0:T(8,128)(2,1)} %refs_1_.1, bf16[128,1024]{1,0:T(8,128)(2,1)} %refs_2_.1, bf16[128,4096]{1,0:T(8,128)(2,1)} %refs_3_.1, s32[2,512]{1,0:T(2,128)} %bitcast.1, ...), custom_call_target="tpu_custom_call" | custom-call | tf_op jit(solution)/shard_map/pallas_call | solution.py:213
  47.2 1.2 %shard_map.86 = (bf16[1024,512]{1,0:T(8,128)(2,1)}, bf16[1024,128]{1,0:T(8,128)(2,1)}, bf16[1024,128]{1,0:T(8,128)(2,1)}) custom-call(bf16[1024,512]{1,0:T(8,128)(2,1)S(1)} %get-tuple-element.6.refs_0_, bf16[1024,128]{1,0:T(8,128)(2,1)S(1)} %get-tuple-element.7.refs_1_, bf16[1024,128]{1,0:T(8,128)(2,1)S(1)} %get-tuple-element.8.refs_2_), custom_call_target="tpu_custom_call" | custom-call | tf_op jit(solution)/shard_map/pallas_call | solution.py:240
